TPU v7x, 128 devices: a whole 4x4x4 slice. The times are simulated.
128 devices in a mesh: lat: 8 (over y_lo, x), lon: 16 (over y_hi, z, core).
Axes of the slice: x: 4, y: 4 (y_hi: 2, y_lo: 2; y = y_hi * 2 + y_lo), z: 4, core: 2. Of those that a mesh axis runs over, the one named last changes fastest.
Arguments:
- latents: bfloat16 [16384, 256], P(('lat', 'lon')), may hold values from -6 to 6
- in_proj: bfloat16 [256, 128], replicated, may hold values from -0.375 to 0.375
- kernel_one: bfloat16 [3, 3, 128, 128], replicated, may hold values from -0.1875 to 0.1875
- kernel_two: bfloat16 [3, 3, 128, 128], replicated, may hold values from -0.1875 to 0.1875
- kernel_three: bfloat16 [3, 3, 128, 128], replicated, may hold values from -0.1875 to 0.1875
- out_proj: bfloat16 [128, 71], replicated, may hold values from -0.5 to 0.5
- bank: bfloat16 [32, 256, 128], replicated, may hold values from -0.375 to 0.375
- obs_values: float32 [4096, 71, 128], P(('lat', 'lon')), may hold values from -6 to 6
- obs_scale: float32 [71], replicated, may hold values from 0.5 to 2
- owner_col: int32 [4096, 1], P(('lat', 'lon')), may hold values from 0 to 15; in each aligned block of 32 rows (0 to 31, 32 to 63, ...) at most 4 rows name the same one
- patch_id: int32 [4096], P(('lat', 'lon')), may hold values from 0 to 7
- bank_id: int32 [4096], P(('lat', 'lon')), may hold values from 0 to 31
Outputs:
- latent_gradient: float32 [16384, 256], P(('lat', 'lon'))
Inputs may be any that keep to these rules, and one draw needn't show every extreme that they name: Block k is held by device k // 32 of lat+lon; its owner tile is in that device's tile row. Among the 32 blocks of one device at most 4 have the same owner_col.
All inputs are finite; a program needn't handle non-finite values.
Results may differ from a plain program's by a relative error of at most 0.011.
Values may be sent and summed in bfloat16 or wider, within the bound.
A program may use at most 64 MiB of HBM per device.

v0:
```python
import functools

import jax
import jax.numpy as jnp
from jax import lax
from jax.experimental import pallas as pl
from jax.experimental.pallas import tpu as pltpu
from jax.sharding import PartitionSpec as P

F32 = jnp.float32
BF16 = jnp.bfloat16
I32 = jnp.int32
MESH = pl.DeviceIdType.MESH
CAP = 4
LW = 8
W = 128
VP = 72
MP = 24
LP = 16
GUARD = 3
HALO = [(-1, -1), (-1, 0), (-1, 1), (0, -1), (0, 1), (1, -1), (1, 0), (1, 1)]


def dot(x, y):
    return jnp.dot(x, y, preferred_element_type=F32)


def dot_nt(x, y):
    return lax.dot_general(x, y, (((1,), (1,)), ((), ())), preferred_element_type=F32)


def shifted(x, by):
    return x if by == 0 else pltpu.roll(x, (-by) % x.shape[0], 0)


def logistic(x):
    return 0.5 * jnp.tanh(0.5 * x) + 0.5


def rounded(x):
    return x.astype(BF16).astype(F32)


TAPS = [(1, -1), (0, 0), (1, 0), (0, 1)]


def window(src, first, count, pitch):
    planes = []
    for p, dr in TAPS:
        line = []
        for q, dc in TAPS:
            at = pl.multiple_of((first + dr) * pitch, 8)
            line.append(shifted(src[2 * q + p, pl.ds(at, count * pitch), :], dc).astype(BF16))
        planes.append(line)
    return planes


def up_weights(k_ref, out_ref):
    rows = {(0, 0): [0], (0, 1): [1, 2], (0, 2): [], (1, 0): [], (1, 1): [0, 1], (1, 2): [2]}
    cols = {(0, 0): [0], (0, 1): [1, 2], (1, 0): [0, 1], (1, 1): [2]}
    for q in range(2):
        for rr in range(3):
            for cc in range(2):
                for p in range(2):
                    block = jnp.zeros((W, W), F32)
                    for i in rows[p, rr]:
                        for j in cols[q, cc]:
                            block = block + k_ref[i, j].astype(F32)
                    at = (rr * 2 + cc) * W
                    out_ref[q, at : at + W, p * W : (p + 1) * W] = block.astype(BF16)


def pair_weights(k_ref, out_ref, flip):
    for m in range(4):
        for j in range(3):
            at = (m * 3 + j) * W
            for p in range(2):
                i = m - p
                if 0 <= i <= 2:
                    block = k_ref[2 - i, 2 - j].astype(F32).T if flip else k_ref[i, j].astype(F32)
                else:
                    block = jnp.zeros((W, W), F32)
                out_ref[at : at + W, p * W : (p + 1) * W] = block.astype(BF16)


def down_weights(k_ref, out_ref):
    for m in range(4):
        for n in range(4):
            block = jnp.zeros((W, W), F32)
            for i in (m - 1, m):
                for j in (n - 1, n):
                    if 0 <= i <= 2 and 0 <= j <= 2:
                        block = block + k_ref[2 - i, 2 - j].astype(F32)
            at = (m * 4 + n) * W
            out_ref[at : at + W, :] = block.T.astype(BF16)


def kernel(
    n_lat,
    n_lon,
    lat_ref,
    inp_ref,
    k1_ref,
    k2_ref,
    k3_ref,
    outp_ref,
    bank_hbm,
    obs_hbm,
    scale_ref,
    owner_ref,
    patch_ref,
    bankid_ref,
    out_ref,
    bank,
    obs,
    row_x,
    sbuf,
    srecv,
    meta_v,
    idx_s,
    meta_s,
    tmp,
    sv,
    rv,
    wu1,
    wu2,
    w3,
    b3,
    wd1,
    wd2,
    opt,
    opad,
    w2,
    f1s,
    d1s,
    f1,
    sl1,
    f2,
    sl2,
    act2,
    sl3,
    actp,
    ft,
    hist,
    ga,
    a3,
    a2,
    ds2,
    b1,
    m1,
    a1,
    zbuf,
    zs,
    zr,
    ctmp,
    ns_s,
    ns_r,
    ew_s,
    ew_r,
    co_s,
    co_r,
    dma_sem,
    st_send,
    st_recv,
    me_send,
    me_recv,
    ob_send,
    ob_recv,
    ha_send,
    ha_recv,
    z_send,
    z_recv,
):
    a, b = lax.axis_index("lat"), lax.axis_index("lon")
    LR = n_lon
    MR = 2 * LR
    npatch = (4 * LR * 4 * LW) // bank.shape[1]
    plen = bank.shape[1]
    nblk = obs.shape[0]
    nvar = obs.shape[1]
    up, down = a > 0, a < n_lat - 1
    upi, downi = jnp.where(up, 1, 0), jnp.where(down, 1, 0)
    first_two, last_two = b < 2, b >= n_lon - 2

    bank_copy = pltpu.make_async_copy(bank_hbm, bank, dma_sem.at[0])
    obs_copy = pltpu.make_async_copy(obs_hbm, obs, dma_sem.at[1])
    obs_copy.start()
    bank_copy.start()
    for row in (0, 1, LR + 2, LR + 3):
        srecv[row] = jnp.zeros((LP, W), BF16)

    barrier = pltpu.get_barrier_semaphore()

    def greet(i, j):
        pl.semaphore_signal(barrier, inc=1, device_id=(i, j), device_id_type=MESH)

    def greet_row(t, c):
        greet(a, lax.rem(b + t, n_lon))
        return c

    lax.fori_loop(1, n_lon, greet_row, 0)

    @pl.when(up)
    def _():
        greet(a - 1, n_lon - 2)
        greet(a - 1, n_lon - 1)
        for d in range(3):
            greet(a - 1, lax.rem(b + n_lon - 1 + d, n_lon))

    @pl.when(down)
    def _():
        greet(a + 1, 0)
        greet(a + 1, 1)
        for d in range(3):
            greet(a + 1, lax.rem(b + n_lon - 1 + d, n_lon))

    feat = rounded(dot(lat_ref[...], inp_ref[...]))
    n_col = n_lon * LW
    row_x[0:8] = feat[n_col - 8 :]
    row_x[8 : 8 + n_col] = feat
    row_x[8 + n_col : 16 + n_col] = feat[0:8]
    for t in range(n_lon):
        sbuf[t] = row_x[8 * t + 4 : 8 * t + 20].astype(BF16)

    lane = lax.broadcasted_iota(I32, (nblk, W), 1)
    sub = lax.broadcasted_iota(I32, (nblk, W), 0)
    eye = lane == sub
    own_c = jnp.broadcast_to(owner_ref[...], (nblk, W))
    own_r = jnp.sum(jnp.where(eye, own_c, 0), axis=0, keepdims=True)
    earlier = jnp.where((own_c == own_r) & (lane < sub), 1, 0)
    rank = jnp.sum(earlier, axis=1, keepdims=True)
    slot = own_c * CAP + rank
    pick = lane == slot

    def column(row_ref):
        row = jnp.broadcast_to(row_ref[...], (nblk, nblk))
        return jnp.sum(jnp.where(eye[:, :nblk], row, 0), axis=1, keepdims=True)

    def per_slot(value):
        return jnp.sum(jnp.where(pick, value, 0), axis=0, keepdims=True)

    rows8 = lax.broadcasted_iota(I32, (8, W), 0)
    meta = jnp.where(rows8 == 0, per_slot(sub), 0)
    meta = jnp.where(rows8 == 1, per_slot(jnp.broadcast_to(column(patch_ref), (nblk, W))), meta)
    meta = jnp.where(rows8 == 2, per_slot(jnp.broadcast_to(column(bankid_ref), (nblk, W))), meta)
    meta = jnp.where(rows8 == 3, per_slot(jnp.ones_like(sub)), meta)
    meta_v[b] = meta
    idx_copy = pltpu.make_async_copy(meta_v.at[b], idx_s, dma_sem.at[2])
    idx_copy.start()

    expected = (
        n_lon - 1
        + jnp.where(first_two & up, n_lon, 0)
        + jnp.where(last_two & down, n_lon, 0)
        + 3 * upi
        + 3 * downi
    )
    pl.semaphore_wait(barrier, expected)

    def row_copy(i, t, at, sem):
        return pltpu.make_async_remote_copy(
            src_ref=sbuf.at[t],
            dst_ref=srecv.at[at],
            send_sem=st_send.at[sem],
            recv_sem=st_recv.at[at],
            device_id=(i, t),
            device_id_type=MESH,
        )

    def send_row(s, c):
        t = lax.rem(b + s, n_lon)
        row_copy(a, t, b + 2, t).start()
        return c

    @pl.when(first_two & up)
    def _():
        def go(t, c):
            row_copy(a - 1, t, LR + 2 + b, n_lon + t).start()
            return c

        lax.fori_loop(0, n_lon, go, 0)

    @pl.when(last_two & down)
    def _():
        def go(t, c):
            row_copy(a + 1, t, b - (n_lon - 2), n_lon + t).start()
            return c

        lax.fori_loop(0, n_lon, go, 0)

    lax.fori_loop(1, n_lon, send_row, 0)
    srecv[b + 2] = sbuf[b]

    def meta_copy(t, slot_at):
        return pltpu.make_async_remote_copy(
            src_ref=meta_v.at[b],
            dst_ref=meta_v.at[slot_at],
            send_sem=me_send.at[t],
            recv_sem=me_recv.at[slot_at],
            device_id=(a, t),
            device_id_type=MESH,
        )

    def send_meta(s, c):
        meta_copy(lax.rem(b + s, n_lon), b).start()
        return c

    lax.fori_loop(1, n_lon, send_meta, 0)

    def obs_copy_to(t, slot_at):
        return pltpu.make_async_remote_copy(
            src_ref=sv.at[t],
            dst_ref=rv.at[slot_at],
            send_sem=ob_send.at[t],
            recv_sem=ob_recv.at[slot_at],
            device_id=(a, t),
            device_id_type=MESH,
        )

    tmp[...] = jnp.zeros_like(tmp)
    obs_copy.wait()
    idx_copy.wait()

    def gathered(t):
        for k in range(CAP):
            tmp[pl.ds(k * VP, nvar), :] = obs[idx_s[0, t * CAP + k]]
        return tmp[...].astype(BF16)

    def send_obs(s, c):
        t = lax.rem(b + s, n_lon)
        sv[t] = gathered(t)
        obs_copy_to(t, b).start()
        return c

    lax.fori_loop(1, n_lon, send_obs, 0)
    rv[b] = gathered(b)

    up_weights(k1_ref, wu1)
    up_weights(k2_ref, wu2)
    pair_weights(k3_ref, w3, False)
    pair_weights(k3_ref, b3, True)
    down_weights(k2_ref, wd2)
    down_weights(k1_ref, wd1)
    opad[...] = jnp.zeros_like(opad)
    opad[:, 0:nvar] = outp_ref[...].astype(F32)
    opt[...] = opad[...].T[0:VP].astype(BF16)
    vlane = lax.broadcasted_iota(I32, (VP, nvar), 1)
    vsub = lax.broadcasted_iota(I32, (VP, nvar), 0)
    scale = jnp.broadcast_to(scale_ref[...], (VP, nvar))
    scale = jnp.sum(jnp.where(vlane == vsub, scale, 0.0), axis=1, keepdims=True)
    w2[...] = jnp.broadcast_to(scale * scale, (VP, W))
    for ref in (f1, sl1, m1, b1):
        ref[...] = jnp.zeros_like(ref)
    for ref in (a3, a2):
        ref[...] = jnp.zeros_like(ref)

    def wait_row(s, c):
        at = lax.rem(b + s, n_lon) + 2
        row_copy(a, b, at, 0).wait_recv()
        return c

    lax.fori_loop(1, n_lon, wait_row, 0)

    @pl.when(up)
    def _():
        row_copy(a, b, 0, 0).wait_recv()
        row_copy(a, b, 1, 0).wait_recv()

    @pl.when(down)
    def _():
        row_copy(a, b, LR + 2, 0).wait_recv()
        row_copy(a, b, LR + 3, 0).wait_recv()

    def inside(first, count, pitch, size):
        row = lax.broadcasted_iota(I32, (count, pitch, W), 0) + first
        low = jnp.where(up, -8, 0)
        high = jnp.where(down, size + 8, size)
        return jnp.where((row >= low) & (row < high), 1.0, 0.0).reshape(count * pitch, W)

    def lifted(line, weights):
        left = [shifted(x, -1).astype(BF16) for x in line]
        here = [x.astype(BF16) for x in line]
        right = [shifted(x, 1).astype(BF16) for x in line]
        phases = []
        for q, (u, v) in enumerate(((left, here), (here, right))):
            x = jnp.concatenate([u[0], v[0], u[1], v[1], u[2], v[2]], axis=1)
            y = dot(x, weights[q])
            phases += [y[:, :W], y[:, W:]]
        return phases

    n1 = LR + 2
    line = [srecv[pl.ds(i, n1)].astype(F32).reshape(n1 * LP, W) for i in range(3)]
    mask = inside(-1, n1, LP, LR)
    for ph, pre in enumerate(lifted(line, wu1)):
        s = logistic(pre)
        f1s[ph] = mask * rounded(pre * s + line[1])
        d1s[ph] = mask * (s * (1.0 + pre * (1.0 - s)))

    def spread(i, c):
        for q in range(2):
            for p in range(2):
                to = pl.ds((2 * i + p + 1) * MP + q, 10, stride=2)
                frm = pl.ds(i * LP + 3, 10)
                f1[to, :] = f1s[2 * q + p, frm, :]
                sl1[to, :] = d1s[2 * q + p, frm, :]
        return c

    lax.fori_loop(0, n1, spread, 0)

    def level_two(i, c):
        first = i * 6 + GUARD - 2
        line = [f1[pl.ds(pl.multiple_of((first + d) * MP, 8), 6 * MP), :] for d in (-1, 0, 1)]
        mask = inside(first - GUARD, 6, MP, MR)
        at = pl.ds(pl.multiple_of(first * MP, 8), 6 * MP)
        for ph, pre in enumerate(lifted(line, wu2)):
            s = logistic(pre)
            f2[ph, at, :] = mask * (pre * s + line[1])
            sl2[ph, at, :] = mask * (s * (1.0 + pre * (1.0 - s)))
        return c

    lax.fori_loop(0, (MR + 4) // 6, level_two, 0)

    def paired(planes, weights, q):
        x = jnp.concatenate([planes[m][q + j] for m in range(4) for j in range(3)], axis=1)
        return dot(x, weights[...])

    def head(i, c):
        first = i * 8 + GUARD
        planes = window(f2, first, 8, MP)
        at = pl.ds(pl.multiple_of(first * MP, 8), 8 * MP)
        for q in range(2):
            y = paired(planes, w3, q)
            for p in range(2):
                pre = y[:, p * W : (p + 1) * W]
                s = logistic(pre)
                act2[2 * q + p, at, :] = pre * s
                sl3[2 * q + p, at, :] = s * (1.0 + pre * (1.0 - s))
        return c

    lax.fori_loop(0, MR // 8, head, 0)

    def points(r, c):
        for q in range(2):
            for p in range(2):
                to = pl.ds((2 * r + p) * (4 * LW) + q, 2 * LW, stride=2)
                actp[to, :] = act2[2 * q + p, pl.ds((r + GUARD) * MP + 2, 2 * LW), :]
        return c

    lax.fori_loop(0, MR, points, 0)
    for n in range(npatch):
        ft[n] = dot_nt(opt[...], actp[n * plen : (n + 1) * plen].astype(BF16)).astype(BF16)

    def wait_meta(s, c):
        meta_copy(b, lax.rem(b + s, n_lon)).wait_recv()
        return c

    lax.fori_loop(1, n_lon, wait_meta, 0)
    meta_down = pltpu.make_async_copy(meta_v, meta_s, dma_sem.at[3])
    meta_down.start()
    bank_copy.wait()
    meta_down.wait()
    none = n_lon * CAP
    hist[none] = jnp.zeros((VP, plen), F32)

    def blocks(s, last):
        source = lax.rem(b + n_lon - s, n_lon)

        @pl.when(s > 0)
        def _():
            obs_copy_to(b, source).wait_recv()

        values = rv[source].astype(F32)
        for k in range(CAP):
            patch = meta_s[source, 1, b * CAP + k]
            rows = bank[meta_s[source, 2, b * CAP + k]]
            live = meta_s[source, 3, b * CAP + k].astype(F32)
            predicted = dot(ft[patch], rows)
            adjoint = (w2[...] * live) * (predicted - values[k * VP : (k + 1) * VP])
            grad = dot_nt(adjoint.astype(BF16), rows)
            before = last[0]
            for n in range(1, npatch):
                before = jnp.where(patch == n, last[n], before)
            hist[s * CAP + k] = grad + hist[before]
            last = tuple(jnp.where(patch == n, s * CAP + k, last[n]) for n in range(npatch))
        return last

    last = lax.fori_loop(0, n_lon, blocks, (jnp.int32(none),) * npatch)

    for n in range(npatch):
        grad = hist[last[n]].astype(BF16)
        ga[n * plen : (n + 1) * plen] = lax.dot_general(
            grad, opt[...], (((0,), (0,)), ((), ())), preferred_element_type=F32
        )

    def adjoint_three(r, c):
        at = pl.ds((r + GUARD) * MP + 2, 2 * LW)
        for q in range(2):
            for p in range(2):
                grad = ga[pl.ds((2 * r + p) * (4 * LW) + q, 2 * LW, stride=2), :]
                a3[2 * q + p, at, :] = grad * sl3[2 * q + p, at, :]
        return c

    lax.fori_loop(0, MR, adjoint_three, 0)

    edge_rows = (0, MR - 2)
    edge_cols = (0, 2 * LW - 2)
    for side in range(2):
        for ph in range(4):
            for i in range(2):
                at = (edge_rows[side] + i + GUARD) * MP + 2
                to = (ph * 2 + i) * 2 * LW
                ns_s[side, to : to + 2 * LW] = a3[ph, at : at + 2 * LW, :].astype(BF16)
                at = GUARD * MP + 2 + edge_cols[side] + i
                to = (ph * 2 + i) * MR
                ew_s[side, to : to + MR] = a3[ph, pl.ds(at, MR, stride=MP), :].astype(BF16)
    for v in range(2):
        for h in range(2):
            for ph in range(4):
                for i in range(2):
                    at = (edge_rows[v] + i + GUARD) * MP + 2 + edge_cols[h]
                    ctmp[v * 2 + h, ph * 4 + i * 2 : ph * 4 + i * 2 + 2] = a3[ph, at : at + 2, :]
            co_s[v * 2 + h] = ctmp[v * 2 + h].astype(BF16)

    def halo_copy(k):
        dy, dx = HALO[k]
        v, h = (dy + 1) // 2, (dx + 1) // 2
        if dy == 0:
            src, dst = ew_s.at[h], ew_r.at[1 - h]
        elif dx == 0:
            src, dst = ns_s.at[v], ns_r.at[1 - v]
        else:
            src, dst = co_s.at[v * 2 + h], co_r.at[(1 - v) * 2 + 1 - h]
        return pltpu.make_async_remote_copy(
            src_ref=src,
            dst_ref=dst,
            send_sem=ha_send.at[k],
            recv_sem=ha_recv.at[7 - k],
            device_id=(a + dy, lax.rem(b + n_lon + dx, n_lon)),
            device_id_type=MESH,
        )

    def halo_arrived(k):
        dy, dx = HALO[k]
        v, h = (dy + 1) // 2, (dx + 1) // 2
        if dy == 0:
            ref = ew_r.at[h]
        elif dx == 0:
            ref = ns_r.at[v]
        else:
            ref = co_r.at[v * 2 + h]
        pltpu.make_async_remote_copy(
            src_ref=ref,
            dst_ref=ref,
            send_sem=ha_send.at[k],
            recv_sem=ha_recv.at[k],
            device_id=(a, b),
            device_id_type=MESH,
        ).wait_recv()

    there = {-1: up, 1: down}
    for dy in (-1, 1):

        @pl.when(there[dy])
        def _():
            for k, (ky, _kx) in enumerate(HALO):
                if ky == dy:
                    halo_copy(k).start()

    for k, (ky, _kx) in enumerate(HALO):
        if ky == 0:
            halo_copy(k).start()

    halo_rows = (-2, MR)
    halo_cols = (0, 2 * LW + 2)
    for dy in (-1, 1):

        @pl.when(there[dy])
        def _():
            v = (dy + 1) // 2
            for k, (ky, _kx) in enumerate(HALO):
                if ky == dy:
                    halo_arrived(k)
            for ph in range(4):
                for i in range(2):
                    at = (halo_rows[v] + i + GUARD) * MP + 2
                    frm = (ph * 2 + i) * 2 * LW
                    a3[ph, at : at + 2 * LW, :] = ns_r[v, frm : frm + 2 * LW].astype(F32)
            for h in range(2):
                ctmp[v * 2 + h] = co_r[v * 2 + h].astype(F32)
                for ph in range(4):
                    for i in range(2):
                        at = (halo_rows[v] + i + GUARD) * MP + halo_cols[h]
                        a3[ph, at : at + 2, :] = ctmp[
                            v * 2 + h, ph * 4 + i * 2 : ph * 4 + i * 2 + 2
                        ]

    for k, (ky, kx) in enumerate(HALO):
        if ky == 0:
            h = (kx + 1) // 2
            halo_arrived(k)
            for ph in range(4):
                for i in range(2):
                    frm = (ph * 2 + i) * MR
                    at = GUARD * MP + halo_cols[h] + i
                    a3[ph, pl.ds(at, MR, stride=MP), :] = ew_r[h, frm : frm + MR].astype(F32)

    def back_three(i, c):
        first = i * 6 + GUARD - 2
        planes = window(a3, first, 6, MP)
        at = pl.ds(pl.multiple_of(first * MP, 8), 6 * MP)
        total = jnp.zeros((6 * MP, W), F32)
        for q in range(2):
            y = paired(planes, b3, q)
            for p in range(2):
                back = y[:, p * W : (p + 1) * W]
                a2[2 * q + p, at, :] = back * sl2[2 * q + p, at, :]
                total = total + back
        ds2[at, :] = total
        return c

    lax.fori_loop(0, (MR + 4) // 6, back_three, 0)

    def gathered_down(planes, weights):
        x = jnp.concatenate([planes[m][n] for m in range(4) for n in range(4)], axis=1)
        return dot(x, weights[...])

    def back_two(i, c):
        first = i * 6 + GUARD - 2
        at = pl.ds(pl.multiple_of(first * MP, 8), 6 * MP)
        back = ds2[at, :] + gathered_down(window(a2, first, 6, MP), wd2)
        b1[at, :] = back
        m1[at, :] = back * sl1[at, :]
        return c

    lax.fori_loop(0, (MR + 4) // 6, back_two, 0)

    def gather(i, c):
        total = jnp.zeros((LP, W), F32)
        for q in range(2):
            for p in range(2):
                frm = pl.ds((2 * i + p + 1) * MP + q, LP, stride=2)
                a1[2 * q + p, pl.ds(pl.multiple_of(i * LP, 8), LP), :] = m1[frm, :]
                total = total + b1[frm, :]
        zbuf[pl.ds(pl.multiple_of(i * LP, 8), LP), :] = total
        return c

    lax.fori_loop(0, n1, gather, 0)
    back = zbuf[LP : LP + LR * LP] + gathered_down(window(a1, 1, LR, LP), wd1)
    zbuf[LP : LP + LR * LP] = rounded(back)
    for r in range(LR):
        zs[r] = zbuf[(r + 1) * LP + 1 : (r + 1) * LP + 1 + LW]

    def z_copy(t, slot_at):
        return pltpu.make_async_remote_copy(
            src_ref=zs.at[t],
            dst_ref=zr.at[slot_at],
            send_sem=z_send.at[t],
            recv_sem=z_recv.at[slot_at],
            device_id=(a, t),
            device_id_type=MESH,
        )

    def send_z(s, c):
        z_copy(lax.rem(b + s, n_lon), b).start()
        return c

    lax.fori_loop(1, n_lon, send_z, 0)
    zr[b] = zs[b]

    def sent(s, c):
        t = lax.rem(b + s, n_lon)
        row_copy(a, t, b + 2, t).wait_send()
        meta_copy(t, b).wait_send()
        obs_copy_to(t, b).wait_send()
        return c

    lax.fori_loop(1, n_lon, sent, 0)

    @pl.when((first_two & up) | (last_two & down))
    def _():
        def go(t, c):
            row_copy(a, t, b + 2, n_lon + t).wait_send()
            return c

        lax.fori_loop(0, n_lon, go, 0)

    for dy in (-1, 1):

        @pl.when(there[dy])
        def _():
            for k, (ky, _kx) in enumerate(HALO):
                if ky == dy:
                    halo_copy(k).wait_send()

    for k, (ky, _kx) in enumerate(HALO):
        if ky == 0:
            halo_copy(k).wait_send()

    def finish(s, c):
        t = lax.rem(b + s, n_lon)
        z_copy(t, b).wait_send()
        z_copy(b, t).wait_recv()
        return c

    lax.fori_loop(1, n_lon, finish, 0)
    out_ref[...] = dot_nt(zr[...].reshape(n_col, W).astype(BF16), inp_ref[...])


def per_device(
    n_lat,
    n_lon,
    latents,
    in_proj,
    kernel_one,
    kernel_two,
    kernel_three,
    out_proj,
    bank,
    obs_values,
    obs_scale,
    owner_col,
    patch_id,
    bank_id,
):
    LR = n_lon
    MR = 2 * LR
    npts = 4 * LR * 4 * LW
    plen = bank.shape[1]
    nmid = (MR + 2 * GUARD) * MP
    n1 = LR + 2
    slots = n_lon * CAP
    vmem = pltpu.VMEM
    dma = pltpu.SemaphoreType.DMA
    scratch = [
        vmem(bank.shape, BF16),
        vmem(obs_values.shape, F32),
        vmem((n_lon * LW + 16, W), F32),
        vmem((n_lon, LP, W), BF16),
        vmem((LR + 4, LP, W), BF16),
        vmem((n_lon, 8, W), I32),
        pltpu.SMEM((8, W), I32),
        pltpu.SMEM((n_lon, 8, W), I32),
        vmem((CAP * VP, W), F32),
        vmem((n_lon, CAP * VP, W), BF16),
        vmem((n_lon, CAP * VP, W), BF16),
        vmem((2, 6 * W, 2 * W), BF16),
        vmem((2, 6 * W, 2 * W), BF16),
        vmem((12 * W, 2 * W), BF16),
        vmem((12 * W, 2 * W), BF16),
        vmem((16 * W, W), BF16),
        vmem((16 * W, W), BF16),
        vmem((VP, W), BF16),
        vmem((W, W), F32),
        vmem((VP, W), F32),
        vmem((4, n1 * LP, W), F32),
        vmem((4, n1 * LP, W), F32),
        vmem((nmid, W), F32),
        vmem((nmid, W), F32),
        vmem((4, nmid, W), F32),
        vmem((4, nmid, W), F32),
        vmem((4, nmid, W), F32),
        vmem((4, nmid, W), F32),
        vmem((npts, W), F32),
        vmem((npts // plen, VP, plen), BF16),
        vmem((slots + 1, VP, plen), F32),
        vmem((npts, W), F32),
        vmem((4, nmid, W), F32),
        vmem((4, nmid, W), F32),
        vmem((nmid, W), F32),
        vmem((nmid, W), F32),
        vmem((nmid, W), F32),
        vmem((4, n1 * LP, W), F32),
        vmem((n1 * LP, W), F32),
        vmem((n_lon, LW, W), F32),
        vmem((n_lon, LW, W), F32),
        vmem((4, 16, W), F32),
        vmem((2, 4 * 2 * 2 * LW, W), BF16),
        vmem((2, 4 * 2 * 2 * LW, W), BF16),
        vmem((2, 4 * 2 * MR, W), BF16),
        vmem((2, 4 * 2 * MR, W), BF16),
        vmem((4, 16, W), BF16),
        vmem((4, 16, W), BF16),
        dma((4,)),
        dma((2 * n_lon,)),
        dma((LR + 4,)),
        dma((n_lon,)),
        dma((n_lon,)),
        dma((n_lon,)),
        dma((n_lon,)),
        dma((8,)),
        dma((8,)),
        dma((n_lon,)),
        dma((n_lon,)),
    ]
    here = pl.BlockSpec(memory_space=pltpu.VMEM)
    far = pl.BlockSpec(memory_space=pl.ANY)
    return pl.pallas_call(
        functools.partial(kernel, n_lat, n_lon),
        out_shape=jax.ShapeDtypeStruct((latents.shape[0], latents.shape[1]), F32),
        in_specs=[here] * 6 + [far] * 2 + [here] * 4,
        out_specs=here,
        scratch_shapes=scratch,
        compiler_params=pltpu.CompilerParams(
            collective_id=0, has_side_effects=True, vmem_limit_bytes=56 * 1024 * 1024
        ),
        cost_estimate=pl.CostEstimate(
            flops=5_000_000_000, bytes_accessed=4_000_000, transcendentals=1_000_000
        ),
    )(
        latents,
        in_proj,
        kernel_one,
        kernel_two,
        kernel_three,
        out_proj,
        bank,
        obs_values,
        obs_scale.reshape(1, -1),
        owner_col,
        patch_id.reshape(1, -1),
        bank_id.reshape(1, -1),
    )


def solution(mesh):
    n_lat, n_lon = mesh.shape["lat"], mesh.shape["lon"]
    placed = (
        P(("lat", "lon"), None),
        P(),
        P(),
        P(),
        P(),
        P(),
        P(),
        P(("lat", "lon"), None, None),
        P(),
        P(("lat", "lon"), None),
        P(("lat", "lon")),
        P(("lat", "lon")),
    )
    return jax.shard_map(
        functools.partial(per_device, n_lat, n_lon),
        mesh=mesh,
        in_specs=placed,
        out_specs=P(("lat", "lon"), None),
        check_vma=False,
    )
```

profile of v0, /device:TPU:25, one launch (start us, length us, event | category | flops | bytes accessed | tf_op | source)
XLA Modules:
  0.0 56.6 jit_solution(13633988860116824394)
XLA Ops:
  0.0 1.3 %copy.15.owner_ref = s32[32,1]{1,0:T(8,128)} copy(s32[32,1]{0,1:T(1,128)} %param.21) | data formatting | bytes 256 | tf_op args[9]
  1.3 1.4 %copy.13.outp_ref = bf16[128,71]{1,0:T(8,128)(2,1)} copy(bf16[128,71]{0,1:T(8,128)(2,1)} %param.17) | data formatting | bytes 36352 | tf_op args[5]
  2.8 2.9 %copy.14.obs_hbm = f32[32,71,128]{2,1,0:T(8,128)} copy(f32[32,71,128]{2,0,1:T(8,128)} %param.19) | data formatting | bytes 2326528 | tf_op args[7]
  5.7 49.3 %shard_map.118 = f32[128,256]{1,0:T(8,128)} custom-call(bf16[128,256]{1,0:T(8,128)(2,1)} %lat_ref.1, bf16[256,128]{1,0:T(8,128)(2,1)} %inp_ref.1, bf16[3,3,128,128]{3,2,1,0:T(8,128)(2,1)} %k1_ref.1, bf16[3,3,128,128]{3,2,1,0:T(8,128)(2,1)} %k2_ref.1, bf16[3,3,128,128]{3,2,1,0:T(8,128)(2,1)} %k3_ref.1, bf16[128,71]{1,0:T(8,128)(2,1)} %copy.13.outp_ref, ...), custom_call_target="tpu_custom_call" | custom-call | flops 5000000000 | bytes 4000000 | tf_op jit(solution)/shard_map/pallas_call | solution.py:797
  55.0 1.6 %copy.17 = f32[128,256]{1,0:T(8,128)} copy(f32[128,256]{1,0:T(8,128)} %shard_map.118) | data formatting | bytes 262144
where the time goes:
time: 56.8 us; the launch traced here: 56.6 us
  Pallas kernels  49.3 us (87%)
  local copies, waits for them, and re-layouts  7.29 us (13%)
    pallas_call x1, Pallas kernels, per_device(): pl.pallas_call(functools.partial(kernel, n_lat, n_lon), out_shape=jax.Sha...  49.3 us
    unnamed x4, local copies, waits for them, and re-layouts  7.29 us

commit v1 on v0

--- a/solution.py
+++ b/solution.py
@@ -17,6 +17,8 @@
 VP = 72
 MP = 24
 LP = 16
+C_TWO, C_HEAD, C_B3, C_B2 = 6, 8, 6, 6
+PARTS = 4
 GUARD = 3
 HALO = [(-1, -1), (-1, 0), (-1, 1), (0, -1), (0, 1), (1, -1), (1, 0), (1, 1)]
 
@@ -98,19 +100,29 @@
 def kernel(
     n_lat,
     n_lon,
+    lat_hbm,
+    inp_hbm,
+    k1_hbm,
+    k2_hbm,
+    k3_hbm,
+    outp_hbm,
+    bank_hbm,
+    obs_hbm,
+    scale_hbm,
+    owner_hbm,
+    patch_hbm,
+    bankid_hbm,
+    out_ref,
     lat_ref,
     inp_ref,
     k1_ref,
     k2_ref,
     k3_ref,
     outp_ref,
-    bank_hbm,
-    obs_hbm,
     scale_ref,
     owner_ref,
     patch_ref,
     bankid_ref,
-    out_ref,
     bank,
     obs,
     row_x,
@@ -141,6 +153,7 @@
     sl3,
     actp,
     ft,
+    pred,
     hist,
     ga,
     a3,
@@ -176,16 +189,12 @@
     MR = 2 * LR
     npatch = (4 * LR * 4 * LW) // bank.shape[1]
     plen = bank.shape[1]
-    nblk = obs.shape[0]
-    nvar = obs.shape[1]
+    nblk = patch_ref.shape[1]
+    nvar = outp_ref.shape[0]
     up, down = a > 0, a < n_lat - 1
     upi, downi = jnp.where(up, 1, 0), jnp.where(down, 1, 0)
     first_two, last_two = b < 2, b >= n_lon - 2
 
-    bank_copy = pltpu.make_async_copy(bank_hbm, bank, dma_sem.at[0])
-    obs_copy = pltpu.make_async_copy(obs_hbm, obs, dma_sem.at[1])
-    obs_copy.start()
-    bank_copy.start()
     for row in (0, 1, LR + 2, LR + 3):
         srecv[row] = jnp.zeros((LP, W), BF16)
 
@@ -214,6 +223,33 @@
         for d in range(3):
             greet(a + 1, lax.rem(b + n_lon - 1 + d, n_lon))
 
+    def local(src, dst, sem):
+        copy = pltpu.make_async_copy(src, dst, dma_sem.at[sem])
+        copy.start()
+        return copy
+
+    row_parts = [local(lat_hbm, lat_ref, 2), local(inp_hbm, inp_ref, 3)]
+    id_parts = [
+        local(owner_hbm, owner_ref, 4),
+        local(patch_hbm, patch_ref, 5),
+        local(bankid_hbm, bankid_ref, 6),
+    ]
+    obs_rows = obs.shape[0] // PARTS
+    bank_rows = bank.shape[0] // PARTS
+    cuts = [pl.ds(i * obs_rows, obs_rows) for i in range(PARTS)]
+    obs_parts = [local(obs_hbm.at[c], obs.at[c], 12 + i) for i, c in enumerate(cuts)]
+    weight_parts = [
+        local(k1_hbm, k1_ref, 7),
+        local(k2_hbm, k2_ref, 8),
+        local(k3_hbm, k3_ref, 9),
+        local(outp_hbm, outp_ref, 10),
+        local(scale_hbm, scale_ref, 11),
+    ]
+    cuts = [pl.ds(i * bank_rows, bank_rows) for i in range(PARTS)]
+    bank_parts = [local(bank_hbm.at[c], bank.at[c], 12 + PARTS + i) for i, c in enumerate(cuts)]
+
+    for part in row_parts:
+        part.wait()
     feat = rounded(dot(lat_ref[...], inp_ref[...]))
     n_col = n_lon * LW
     row_x[0:8] = feat[n_col - 8 :]
@@ -222,19 +258,22 @@
     for t in range(n_lon):
         sbuf[t] = row_x[8 * t + 4 : 8 * t + 20].astype(BF16)
 
+    for part in id_parts:
+        part.wait()
     lane = lax.broadcasted_iota(I32, (nblk, W), 1)
     sub = lax.broadcasted_iota(I32, (nblk, W), 0)
     eye = lane == sub
-    own_c = jnp.broadcast_to(owner_ref[...], (nblk, W))
+
+    def column(row_ref):
+        row = jnp.broadcast_to(row_ref[...], (nblk, nblk))
+        return jnp.sum(jnp.where(eye[:, :nblk], row, 0), axis=1, keepdims=True)
+
+    own_c = jnp.broadcast_to(column(owner_ref), (nblk, W))
     own_r = jnp.sum(jnp.where(eye, own_c, 0), axis=0, keepdims=True)
     earlier = jnp.where((own_c == own_r) & (lane < sub), 1, 0)
     rank = jnp.sum(earlier, axis=1, keepdims=True)
     slot = own_c * CAP + rank
     pick = lane == slot
-
-    def column(row_ref):
-        row = jnp.broadcast_to(row_ref[...], (nblk, nblk))
-        return jnp.sum(jnp.where(eye[:, :nblk], row, 0), axis=1, keepdims=True)
 
     def per_slot(value):
         return jnp.sum(jnp.where(pick, value, 0), axis=0, keepdims=True)
@@ -245,7 +284,7 @@
     meta = jnp.where(rows8 == 2, per_slot(jnp.broadcast_to(column(bankid_ref), (nblk, W))), meta)
     meta = jnp.where(rows8 == 3, per_slot(jnp.ones_like(sub)), meta)
     meta_v[b] = meta
-    idx_copy = pltpu.make_async_copy(meta_v.at[b], idx_s, dma_sem.at[2])
+    idx_copy = pltpu.make_async_copy(meta_v.at[b], idx_s, dma_sem.at[0])
     idx_copy.start()
 
     expected = (
@@ -318,12 +357,14 @@
         )
 
     tmp[...] = jnp.zeros_like(tmp)
-    obs_copy.wait()
+    for part in obs_parts:
+        part.wait()
     idx_copy.wait()
 
     def gathered(t):
         for k in range(CAP):
-            tmp[pl.ds(k * VP, nvar), :] = obs[idx_s[0, t * CAP + k]]
+            block = pl.ds(idx_s[0, t * CAP + k], nvar, stride=nblk)
+            tmp[pl.ds(k * VP, nvar), :] = obs[block, :]
         return tmp[...].astype(BF16)
 
     def send_obs(s, c):
@@ -335,6 +376,8 @@
     lax.fori_loop(1, n_lon, send_obs, 0)
     rv[b] = gathered(b)
 
+    for part in weight_parts:
+        part.wait()
     up_weights(k1_ref, wu1)
     up_weights(k2_ref, wu2)
     pair_weights(k3_ref, w3, False)
@@ -342,8 +385,8 @@
     down_weights(k2_ref, wd2)
     down_weights(k1_ref, wd1)
     opad[...] = jnp.zeros_like(opad)
-    opad[:, 0:nvar] = outp_ref[...].astype(F32)
-    opt[...] = opad[...].T[0:VP].astype(BF16)
+    opad[0:nvar] = outp_ref[...].astype(F32)
+    opt[...] = opad[...].astype(BF16)
     vlane = lax.broadcasted_iota(I32, (VP, nvar), 1)
     vsub = lax.broadcasted_iota(I32, (VP, nvar), 0)
     scale = jnp.broadcast_to(scale_ref[...], (VP, nvar))
@@ -408,26 +451,26 @@
     lax.fori_loop(0, n1, spread, 0)
 
     def level_two(i, c):
-        first = i * 6 + GUARD - 2
-        line = [f1[pl.ds(pl.multiple_of((first + d) * MP, 8), 6 * MP), :] for d in (-1, 0, 1)]
-        mask = inside(first - GUARD, 6, MP, MR)
-        at = pl.ds(pl.multiple_of(first * MP, 8), 6 * MP)
+        first = i * C_TWO + GUARD - 2
+        line = [f1[pl.ds(pl.multiple_of((first + d) * MP, 8), C_TWO * MP), :] for d in (-1, 0, 1)]
+        mask = inside(first - GUARD, C_TWO, MP, MR)
+        at = pl.ds(pl.multiple_of(first * MP, 8), C_TWO * MP)
         for ph, pre in enumerate(lifted(line, wu2)):
             s = logistic(pre)
             f2[ph, at, :] = mask * (pre * s + line[1])
             sl2[ph, at, :] = mask * (s * (1.0 + pre * (1.0 - s)))
         return c
 
-    lax.fori_loop(0, (MR + 4) // 6, level_two, 0)
+    lax.fori_loop(0, (MR + 4) // C_TWO, level_two, 0)
 
     def paired(planes, weights, q):
         x = jnp.concatenate([planes[m][q + j] for m in range(4) for j in range(3)], axis=1)
         return dot(x, weights[...])
 
     def head(i, c):
-        first = i * 8 + GUARD
-        planes = window(f2, first, 8, MP)
-        at = pl.ds(pl.multiple_of(first * MP, 8), 8 * MP)
+        first = i * C_HEAD + GUARD
+        planes = window(f2, first, C_HEAD, MP)
+        at = pl.ds(pl.multiple_of(first * MP, 8), C_HEAD * MP)
         for q in range(2):
             y = paired(planes, w3, q)
             for p in range(2):
@@ -437,7 +480,7 @@
                 sl3[2 * q + p, at, :] = s * (1.0 + pre * (1.0 - s))
         return c
 
-    lax.fori_loop(0, MR // 8, head, 0)
+    lax.fori_loop(0, MR // C_HEAD, head, 0)
 
     def points(r, c):
         for q in range(2):
@@ -455,13 +498,23 @@
         return c
 
     lax.fori_loop(1, n_lon, wait_meta, 0)
-    meta_down = pltpu.make_async_copy(meta_v, meta_s, dma_sem.at[3])
+    meta_down = pltpu.make_async_copy(meta_v, meta_s, dma_sem.at[1])
     meta_down.start()
-    bank_copy.wait()
+    for part in bank_parts:
+        part.wait()
     meta_down.wait()
     none = n_lon * CAP
     hist[none] = jnp.zeros((VP, plen), F32)
 
+    def predict(s, c):
+        source = lax.rem(b + n_lon - s, n_lon)
+        for k in range(CAP):
+            rows = bank[meta_s[source, 2, b * CAP + k]]
+            pred[s * CAP + k] = dot(ft[meta_s[source, 1, b * CAP + k]], rows)
+        return c
+
+    lax.fori_loop(0, n_lon, predict, 0)
+
     def blocks(s, last):
         source = lax.rem(b + n_lon - s, n_lon)
 
@@ -470,17 +523,18 @@
             obs_copy_to(b, source).wait_recv()
 
         values = rv[source].astype(F32)
+        grads = []
+        for k in range(CAP):
+            rows = bank[meta_s[source, 2, b * CAP + k]]
+            live = meta_s[source, 3, b * CAP + k].astype(F32)
+            adjoint = (w2[...] * live) * (pred[s * CAP + k] - values[k * VP : (k + 1) * VP])
+            grads.append(dot_nt(adjoint.astype(BF16), rows))
         for k in range(CAP):
             patch = meta_s[source, 1, b * CAP + k]
-            rows = bank[meta_s[source, 2, b * CAP + k]]
-            live = meta_s[source, 3, b * CAP + k].astype(F32)
-            predicted = dot(ft[patch], rows)
-            adjoint = (w2[...] * live) * (predicted - values[k * VP : (k + 1) * VP])
-            grad = dot_nt(adjoint.astype(BF16), rows)
             before = last[0]
             for n in range(1, npatch):
                 before = jnp.where(patch == n, last[n], before)
-            hist[s * CAP + k] = grad + hist[before]
+            hist[s * CAP + k] = grads[k] + hist[before]
             last = tuple(jnp.where(patch == n, s * CAP + k, last[n]) for n in range(npatch))
         return last
 
@@ -605,10 +659,10 @@
                     a3[ph, pl.ds(at, MR, stride=MP), :] = ew_r[h, frm : frm + MR].astype(F32)
 
     def back_three(i, c):
-        first = i * 6 + GUARD - 2
-        planes = window(a3, first, 6, MP)
-        at = pl.ds(pl.multiple_of(first * MP, 8), 6 * MP)
-        total = jnp.zeros((6 * MP, W), F32)
+        first = i * C_B3 + GUARD - 2
+        planes = window(a3, first, C_B3, MP)
+        at = pl.ds(pl.multiple_of(first * MP, 8), C_B3 * MP)
+        total = jnp.zeros((C_B3 * MP, W), F32)
         for q in range(2):
             y = paired(planes, b3, q)
             for p in range(2):
@@ -618,21 +672,21 @@
         ds2[at, :] = total
         return c
 
-    lax.fori_loop(0, (MR + 4) // 6, back_three, 0)
+    lax.fori_loop(0, (MR + 4) // C_B3, back_three, 0)
 
     def gathered_down(planes, weights):
         x = jnp.concatenate([planes[m][n] for m in range(4) for n in range(4)], axis=1)
         return dot(x, weights[...])
 
     def back_two(i, c):
-        first = i * 6 + GUARD - 2
-        at = pl.ds(pl.multiple_of(first * MP, 8), 6 * MP)
-        back = ds2[at, :] + gathered_down(window(a2, first, 6, MP), wd2)
+        first = i * C_B2 + GUARD - 2
+        at = pl.ds(pl.multiple_of(first * MP, 8), C_B2 * MP)
+        back = ds2[at, :] + gathered_down(window(a2, first, C_B2, MP), wd2)
         b1[at, :] = back
         m1[at, :] = back * sl1[at, :]
         return c
 
-    lax.fori_loop(0, (MR + 4) // 6, back_two, 0)
+    lax.fori_loop(0, (MR + 4) // C_B2, back_two, 0)
 
     def gather(i, c):
         total = jnp.zeros((LP, W), F32)
@@ -703,7 +757,7 @@
         return c
 
     lax.fori_loop(1, n_lon, finish, 0)
-    out_ref[...] = dot_nt(zr[...].reshape(n_col, W).astype(BF16), inp_ref[...])
+    out_ref[...] = zr[...].reshape(n_col, W).astype(BF16)
 
 
 def per_device(
@@ -731,9 +785,20 @@
     slots = n_lon * CAP
     vmem = pltpu.VMEM
     dma = pltpu.SemaphoreType.DMA
+    nvar, nblk = obs_values.shape[1], obs_values.shape[0]
     scratch = [
+        vmem(latents.shape, BF16),
+        vmem(in_proj.shape, BF16),
+        vmem(kernel_one.shape, BF16),
+        vmem(kernel_two.shape, BF16),
+        vmem(kernel_three.shape, BF16),
+        vmem((nvar, W), BF16),
+        vmem((1, nvar), F32),
+        vmem((1, nblk), I32),
+        vmem((1, nblk), I32),
+        vmem((1, nblk), I32),
         vmem(bank.shape, BF16),
-        vmem(obs_values.shape, F32),
+        vmem((obs_values.shape[0] * obs_values.shape[1], W), F32),
         vmem((n_lon * LW + 16, W), F32),
         vmem((n_lon, LP, W), BF16),
         vmem((LR + 4, LP, W), BF16),
@@ -750,7 +815,7 @@
         vmem((16 * W, W), BF16),
         vmem((16 * W, W), BF16),
         vmem((VP, W), BF16),
-        vmem((W, W), F32),
+        vmem((VP, W), F32),
         vmem((VP, W), F32),
         vmem((4, n1 * LP, W), F32),
         vmem((4, n1 * LP, W), F32),
@@ -762,6 +827,7 @@
         vmem((4, nmid, W), F32),
         vmem((npts, W), F32),
         vmem((npts // plen, VP, plen), BF16),
+        vmem((slots, VP, W), F32),
         vmem((slots + 1, VP, plen), F32),
         vmem((npts, W), F32),
         vmem((4, nmid, W), F32),
@@ -780,7 +846,7 @@
         vmem((2, 4 * 2 * MR, W), BF16),
         vmem((4, 16, W), BF16),
         vmem((4, 16, W), BF16),
-        dma((4,)),
+        dma((12 + 2 * PARTS,)),
         dma((2 * n_lon,)),
         dma((LR + 4,)),
         dma((n_lon,)),
@@ -794,10 +860,10 @@
     ]
     here = pl.BlockSpec(memory_space=pltpu.VMEM)
     far = pl.BlockSpec(memory_space=pl.ANY)
-    return pl.pallas_call(
+    back_zero = pl.pallas_call(
         functools.partial(kernel, n_lat, n_lon),
-        out_shape=jax.ShapeDtypeStruct((latents.shape[0], latents.shape[1]), F32),
-        in_specs=[here] * 6 + [far] * 2 + [here] * 4,
+        out_shape=jax.ShapeDtypeStruct((latents.shape[0], W), BF16),
+        in_specs=[far] * 12,
         out_specs=here,
         scratch_shapes=scratch,
         compiler_params=pltpu.CompilerParams(
@@ -812,14 +878,15 @@
         kernel_one,
         kernel_two,
         kernel_three,
-        out_proj,
+        out_proj.T,
         bank,
-        obs_values,
+        jnp.transpose(obs_values, (1, 0, 2)).reshape(nvar * nblk, W),
         obs_scale.reshape(1, -1),
-        owner_col,
+        owner_col.reshape(1, -1),
         patch_id.reshape(1, -1),
         bank_id.reshape(1, -1),
     )
+    return dot_nt(back_zero, in_proj)
 
 
 def solution(mesh):

time: 56.8 us -> 46.7 us (0.82)
  local copies, waits for them, and re-layouts: 7.29 us -> 0.01 us
  Pallas kernels: 49.3 us -> 44.9 us
  matrix products: 0 us -> 1.58 us
    unnamed x4 -> x2, local copies, waits for them, and re-layouts: 7.29 us -> 0.01 us
    pallas_call x1, Pallas kernels: 49.3 us -> 44.9 us  [per_device(): pl.pallas_call(functools.partial(kernel, n_lat, n_lon), out_shape=jax.Sha...]
    dot_general x0 -> x1, matrix products: none -> 1.58 us  [dot_nt(): lax.dot_general(x, y, (((1,), (1,)), ((), ())), preferred_element_type=F32)]
where the time goes in v1:
time: 46.7 us; the launch traced here: 46.5 us
  Pallas kernels  44.9 us (96%)
  matrix products  1.58 us (3%)
    pallas_call x1, Pallas kernels, per_device(): pl.pallas_call(functools.partial(kernel, n_lat, n_lon), out_shape=jax.Sha...  44.9 us
    dot_general x1, matrix products, dot_nt(): lax.dot_general(x, y, (((1,), (1,)), ((), ())), preferred_element_type=F32)  1.58 us

profile of v1, /device:TPU:25, one launch (start us, length us, event | category | flops | bytes accessed | tf_op | source)
XLA Modules:
  0.0 46.5 jit_solution(5686062326415372418)
XLA Ops:
  0.0 0.0 copy-start
  0.0 44.9 %shard_map.118 = bf16[128,128]{1,0:T(8,128)(2,1)} custom-call(bf16[128,256]{1,0:T(8,128)(2,1)} %lat_hbm.1, bf16[256,128]{1,0:T(8,128)(2,1)} %inp_hbm.1, bf16[3,3,128,128]{3,2,1,0:T(8,128)(2,1)} %k1_hbm.1, bf16[3,3,128,128]{3,2,1,0:T(8,128)(2,1)} %k2_hbm.1, bf16[3,3,128,128]{3,2,1,0:T(8,128)(2,1)} %k3_hbm.1, bf16[71,128]{1,0:T(8,128)(2,1)} %bitcast.11, ...), custom_call_target="tpu_custom_call" | custom-call | flops 5000000000 | bytes 4000000 | tf_op jit(solution)/shard_map/pallas_call | solution.py:863
  44.9 0.0 copy-done
  45.0 1.6 %fusion = f32[128,256]{1,0:T(8,128)} fusion(bf16[128,128]{1,0:T(8,128)(2,1)} %shard_map.118, bf16[256,128]{1,0:T(8,128)(2,1)S(1)} %copy-done), kind=kOutput, calls=%fused_computation | convolution fusion | flops 8388608 | bytes 229376 | tf_op jit(solution)/shard_map/dot_general | solution.py:31
Async XLA Ops:
  0.0 44.9 %copy-start = (bf16[256,128]{1,0:T(8,128)(2,1)S(1)}, bf16[256,128]{1,0:T(8,128)(2,1)}, u32[]{:S(2)}) copy-start(bf16[256,128]{1,0:T(8,128)(2,1)} %inp_hbm.1) | copy-start | bytes 196612

commit v2 on v1

--- a/solution.py
+++ b/solution.py
@@ -17,7 +17,7 @@
 VP = 72
 MP = 24
 LP = 16
-C_TWO, C_HEAD, C_B3, C_B2 = 6, 8, 6, 6
+S_TWO, S_HEAD, S_B3, S_B2 = 3, 2, 2, 2
 PARTS = 4
 GUARD = 3
 HALO = [(-1, -1), (-1, 0), (-1, 1), (0, -1), (0, 1), (1, -1), (1, 0), (1, 1)]
@@ -189,12 +189,27 @@
     MR = 2 * LR
     npatch = (4 * LR * 4 * LW) // bank.shape[1]
     plen = bank.shape[1]
+    C_TWO, C_B3, C_B2 = (MR + 4) // S_TWO, (MR + 4) // S_B3, (MR + 4) // S_B2
+    C_HEAD = MR // S_HEAD
     nblk = patch_ref.shape[1]
     nvar = outp_ref.shape[0]
     up, down = a > 0, a < n_lat - 1
     upi, downi = jnp.where(up, 1, 0), jnp.where(down, 1, 0)
     first_two, last_two = b < 2, b >= n_lon - 2
 
+    flips = [bit * (1 - 2 * lax.rem(b // bit, 2)) for bit in (1, 2, 4, 8) if bit < n_lon]
+    groups = n_lon // 4
+    order = range(n_lon - 1, 0, -1)
+
+    def peer(k):
+        return b + sum(flip for i, flip in enumerate(flips) if k >> i & 1)
+
+    def after(t):
+        return b + t - jnp.where(b + t >= n_lon, n_lon, 0)
+
+    def before_me(t):
+        return b - t + jnp.where(b < t, n_lon, 0)
+
     for row in (0, 1, LR + 2, LR + 3):
         srecv[row] = jnp.zeros((LP, W), BF16)
 
@@ -203,11 +218,8 @@
     def greet(i, j):
         pl.semaphore_signal(barrier, inc=1, device_id=(i, j), device_id_type=MESH)
 
-    def greet_row(t, c):
-        greet(a, lax.rem(b + t, n_lon))
-        return c
-
-    lax.fori_loop(1, n_lon, greet_row, 0)
+    for k in order:
+        greet(a, peer(k))
 
     @pl.when(up)
     def _():
@@ -306,10 +318,8 @@
             device_id_type=MESH,
         )
 
-    def send_row(s, c):
-        t = lax.rem(b + s, n_lon)
-        row_copy(a, t, b + 2, t).start()
-        return c
+    for k in order:
+        row_copy(a, peer(k), b + 2, peer(k)).start()
 
     @pl.when(first_two & up)
     def _():
@@ -327,7 +337,6 @@
 
         lax.fori_loop(0, n_lon, go, 0)
 
-    lax.fori_loop(1, n_lon, send_row, 0)
     srecv[b + 2] = sbuf[b]
 
     def meta_copy(t, slot_at):
@@ -340,11 +349,8 @@
             device_id_type=MESH,
         )
 
-    def send_meta(s, c):
-        meta_copy(lax.rem(b + s, n_lon), b).start()
-        return c
-
-    lax.fori_loop(1, n_lon, send_meta, 0)
+    for k in order:
+        meta_copy(peer(k), b).start()
 
     def obs_copy_to(t, slot_at):
         return pltpu.make_async_remote_copy(
@@ -367,13 +373,22 @@
             tmp[pl.ds(k * VP, nvar), :] = obs[block, :]
         return tmp[...].astype(BF16)
 
-    def send_obs(s, c):
-        t = lax.rem(b + s, n_lon)
-        sv[t] = gathered(t)
-        obs_copy_to(t, b).start()
+    def send_obs(g, c):
+        for k in range(4):
+            t = after(g * 4 + k)
+            if k > 0:
+                sv[t] = gathered(t)
+                obs_copy_to(t, b).start()
+            else:
+
+                @pl.when(g > 0)
+                def _():
+                    sv[t] = gathered(t)
+                    obs_copy_to(t, b).start()
+
         return c
 
-    lax.fori_loop(1, n_lon, send_obs, 0)
+    lax.fori_loop(0, groups, send_obs, 0)
     rv[b] = gathered(b)
 
     for part in weight_parts:
@@ -397,12 +412,8 @@
     for ref in (a3, a2):
         ref[...] = jnp.zeros_like(ref)
 
-    def wait_row(s, c):
-        at = lax.rem(b + s, n_lon) + 2
-        row_copy(a, b, at, 0).wait_recv()
-        return c
-
-    lax.fori_loop(1, n_lon, wait_row, 0)
+    for k in order:
+        row_copy(a, b, peer(k) + 2, 0).wait_recv()
 
     @pl.when(up)
     def _():
@@ -449,6 +460,11 @@
         return c
 
     lax.fori_loop(0, n1, spread, 0)
+
+    for k in order:
+        meta_copy(b, peer(k)).wait_recv()
+    meta_down = pltpu.make_async_copy(meta_v, meta_s, dma_sem.at[1])
+    meta_down.start()
 
     def level_two(i, c):
         first = i * C_TWO + GUARD - 2
@@ -493,52 +509,52 @@
     for n in range(npatch):
         ft[n] = dot_nt(opt[...], actp[n * plen : (n + 1) * plen].astype(BF16)).astype(BF16)
 
-    def wait_meta(s, c):
-        meta_copy(b, lax.rem(b + s, n_lon)).wait_recv()
-        return c
-
-    lax.fori_loop(1, n_lon, wait_meta, 0)
-    meta_down = pltpu.make_async_copy(meta_v, meta_s, dma_sem.at[1])
-    meta_down.start()
     for part in bank_parts:
         part.wait()
     meta_down.wait()
     none = n_lon * CAP
     hist[none] = jnp.zeros((VP, plen), F32)
 
-    def predict(s, c):
-        source = lax.rem(b + n_lon - s, n_lon)
-        for k in range(CAP):
-            rows = bank[meta_s[source, 2, b * CAP + k]]
-            pred[s * CAP + k] = dot(ft[meta_s[source, 1, b * CAP + k]], rows)
+    def predict(g, c):
+        for m in range(4):
+            source = before_me(g * 4 + m)
+            for k in range(CAP):
+                rows = bank[meta_s[source, 2, b * CAP + k]]
+                slot_at = (g * 4 + m) * CAP + k
+                pred[slot_at] = dot(ft[meta_s[source, 1, b * CAP + k]], rows)
         return c
 
-    lax.fori_loop(0, n_lon, predict, 0)
-
-    def blocks(s, last):
-        source = lax.rem(b + n_lon - s, n_lon)
-
-        @pl.when(s > 0)
-        def _():
-            obs_copy_to(b, source).wait_recv()
-
-        values = rv[source].astype(F32)
-        grads = []
-        for k in range(CAP):
-            rows = bank[meta_s[source, 2, b * CAP + k]]
-            live = meta_s[source, 3, b * CAP + k].astype(F32)
-            adjoint = (w2[...] * live) * (pred[s * CAP + k] - values[k * VP : (k + 1) * VP])
-            grads.append(dot_nt(adjoint.astype(BF16), rows))
-        for k in range(CAP):
-            patch = meta_s[source, 1, b * CAP + k]
-            before = last[0]
-            for n in range(1, npatch):
-                before = jnp.where(patch == n, last[n], before)
-            hist[s * CAP + k] = grads[k] + hist[before]
-            last = tuple(jnp.where(patch == n, s * CAP + k, last[n]) for n in range(npatch))
+    lax.fori_loop(0, groups, predict, 0)
+
+    def blocks(g, last):
+        for m in range(4):
+            source = before_me(g * 4 + m)
+            if m > 0:
+                obs_copy_to(b, source).wait_recv()
+            else:
+
+                @pl.when(g > 0)
+                def _():
+                    obs_copy_to(b, source).wait_recv()
+
+            values = rv[source].astype(F32)
+            grads = []
+            for k in range(CAP):
+                rows = bank[meta_s[source, 2, b * CAP + k]]
+                live = meta_s[source, 3, b * CAP + k].astype(F32)
+                miss = pred[(g * 4 + m) * CAP + k] - values[k * VP : (k + 1) * VP]
+                grads.append(dot_nt(((w2[...] * live) * miss).astype(BF16), rows))
+            for k in range(CAP):
+                patch = meta_s[source, 1, b * CAP + k]
+                slot_at = (g * 4 + m) * CAP + k
+                before = last[0]
+                for n in range(1, npatch):
+                    before = jnp.where(patch == n, last[n], before)
+                hist[slot_at] = grads[k] + hist[before]
+                last = tuple(jnp.where(patch == n, slot_at, last[n]) for n in range(npatch))
         return last
 
-    last = lax.fori_loop(0, n_lon, blocks, (jnp.int32(none),) * npatch)
+    last = lax.fori_loop(0, groups, blocks, (jnp.int32(none),) * npatch)
 
     for n in range(npatch):
         grad = hist[last[n]].astype(BF16)
@@ -714,21 +730,14 @@
             device_id_type=MESH,
         )
 
-    def send_z(s, c):
-        z_copy(lax.rem(b + s, n_lon), b).start()
-        return c
-
-    lax.fori_loop(1, n_lon, send_z, 0)
+    for k in order:
+        z_copy(peer(k), b).start()
     zr[b] = zs[b]
 
-    def sent(s, c):
-        t = lax.rem(b + s, n_lon)
-        row_copy(a, t, b + 2, t).wait_send()
-        meta_copy(t, b).wait_send()
-        obs_copy_to(t, b).wait_send()
-        return c
-
-    lax.fori_loop(1, n_lon, sent, 0)
+    for k in order:
+        row_copy(a, peer(k), b + 2, peer(k)).wait_send()
+        meta_copy(peer(k), b).wait_send()
+        obs_copy_to(peer(k), b).wait_send()
 
     @pl.when((first_two & up) | (last_two & down))
     def _():
@@ -750,13 +759,9 @@
         if ky == 0:
             halo_copy(k).wait_send()
 
-    def finish(s, c):
-        t = lax.rem(b + s, n_lon)
-        z_copy(t, b).wait_send()
-        z_copy(b, t).wait_recv()
-        return c
-
-    lax.fori_loop(1, n_lon, finish, 0)
+    for k in order:
+        z_copy(peer(k), b).wait_send()
+        z_copy(b, peer(k)).wait_recv()
     out_ref[...] = zr[...].reshape(n_col, W).astype(BF16)
 
 
@@ -862,7 +867,7 @@
     far = pl.BlockSpec(memory_space=pl.ANY)
     back_zero = pl.pallas_call(
         functools.partial(kernel, n_lat, n_lon),
-        out_shape=jax.ShapeDtypeStruct((latents.shape[0], W), BF16),
+        out_shape=pltpu.VMEM((latents.shape[0], W), BF16),
         in_specs=[far] * 12,
         out_specs=here,
         scratch_shapes=scratch,

time: 46.7 us -> 43.7 us (0.936)
  Pallas kernels: 44.9 us -> 42.8 us
  matrix products: 1.58 us -> 0.83 us
    pallas_call x1, Pallas kernels: 44.9 us -> 42.8 us  [per_device(): pl.pallas_call(functools.partial(kernel, n_lat, n_lon), out_shape=pltpu.V...]
    dot_general x1, matrix products: 1.58 us -> 0.83 us  [dot_nt(): lax.dot_general(x, y, (((1,), (1,)), ((), ())), preferred_element_type=F32)]
where the time goes in v2:
time: 43.7 us; the launch traced here: 43.6 us
  Pallas kernels  42.8 us (98%)
  matrix products  0.83 us (2%)
    pallas_call x1, Pallas kernels, per_device(): pl.pallas_call(functools.partial(kernel, n_lat, n_lon), out_shape=pltpu.V...  42.8 us

profile of v2, /device:TPU:25, one launch (start us, length us, event | category | flops | bytes accessed | tf_op | source)
XLA Modules:
  0.0 43.6 jit_solution(8932130672487494928)
XLA Ops:
  0.0 0.0 copy-start
  0.0 42.8 %shard_map.118 = bf16[128,128]{1,0:T(8,128)(2,1)S(1)} custom-call(bf16[128,256]{1,0:T(8,128)(2,1)} %lat_hbm.1, bf16[256,128]{1,0:T(8,128)(2,1)} %inp_hbm.1, bf16[3,3,128,128]{3,2,1,0:T(8,128)(2,1)} %k1_hbm.1, bf16[3,3,128,128]{3,2,1,0:T(8,128)(2,1)} %k2_hbm.1, bf16[3,3,128,128]{3,2,1,0:T(8,128)(2,1)} %k3_hbm.1, bf16[71,128]{1,0:T(8,128)(2,1)} %bitcast.11, ...), custom_call_target="tpu_custom_call" | custom-call | flops 5000000000 | bytes 4000000 | tf_op jit(solution)/shard_map/pallas_call | solution.py:868
  42.8 0.0 copy-done
  42.8 0.8 %fusion = f32[128,256]{1,0:T(8,128)} fusion(bf16[128,128]{1,0:T(8,128)(2,1)S(1)} %shard_map.118, bf16[256,128]{1,0:T(8,128)(2,1)S(1)} %copy-done), kind=kOutput, calls=%fused_computation | convolution fusion | flops 8388608 | bytes 229376 | tf_op jit(solution)/shard_map/dot_general | solution.py:31
Async XLA Ops:
  0.0 42.8 %copy-start = (bf16[256,128]{1,0:T(8,128)(2,1)S(1)}, bf16[256,128]{1,0:T(8,128)(2,1)}, u32[]{:S(2)}) copy-start(bf16[256,128]{1,0:T(8,128)(2,1)} %inp_hbm.1) | copy-start | bytes 196612

commit v3 on v2

--- a/solution.py
+++ b/solution.py
@@ -17,7 +17,7 @@
 VP = 72
 MP = 24
 LP = 16
-S_TWO, S_HEAD, S_B3, S_B2 = 3, 2, 2, 2
+S_TWO, S_HEAD, S_B3, S_B2 = 2, 1, 1, 1
 PARTS = 4
 GUARD = 3
 HALO = [(-1, -1), (-1, 0), (-1, 1), (0, -1), (0, 1), (1, -1), (1, 0), (1, 1)]
@@ -204,6 +204,9 @@
     def peer(k):
         return b + sum(flip for i, flip in enumerate(flips) if k >> i & 1)
 
+    def turn(g, k):
+        return 2 * g + 1 + k // 2 + (k % 2) * (n_lon // 2)
+
     def after(t):
         return b + t - jnp.where(b + t >= n_lon, n_lon, 0)
 
@@ -375,13 +378,13 @@
 
     def send_obs(g, c):
         for k in range(4):
-            t = after(g * 4 + k)
-            if k > 0:
+            t = after(turn(g, k))
+            if k < 3:
                 sv[t] = gathered(t)
                 obs_copy_to(t, b).start()
             else:
 
-                @pl.when(g > 0)
+                @pl.when(g < groups - 1)
                 def _():
                     sv[t] = gathered(t)
                     obs_copy_to(t, b).start()
@@ -459,7 +462,7 @@
                 sl1[to, :] = d1s[2 * q + p, frm, :]
         return c
 
-    lax.fori_loop(0, n1, spread, 0)
+    lax.fori_loop(0, n1, spread, 0, unroll=3)
 
     for k in order:
         meta_copy(b, peer(k)).wait_recv()
@@ -505,7 +508,7 @@
                 actp[to, :] = act2[2 * q + p, pl.ds((r + GUARD) * MP + 2, 2 * LW), :]
         return c
 
-    lax.fori_loop(0, MR, points, 0)
+    lax.fori_loop(0, MR, points, 0, unroll=4)
     for n in range(npatch):
         ft[n] = dot_nt(opt[...], actp[n * plen : (n + 1) * plen].astype(BF16)).astype(BF16)
 
@@ -517,7 +520,7 @@
 
     def predict(g, c):
         for m in range(4):
-            source = before_me(g * 4 + m)
+            source = before_me(turn(g, m))
             for k in range(CAP):
                 rows = bank[meta_s[source, 2, b * CAP + k]]
                 slot_at = (g * 4 + m) * CAP + k
@@ -528,12 +531,12 @@
 
     def blocks(g, last):
         for m in range(4):
-            source = before_me(g * 4 + m)
-            if m > 0:
+            source = before_me(turn(g, m))
+            if m < 3:
                 obs_copy_to(b, source).wait_recv()
             else:
 
-                @pl.when(g > 0)
+                @pl.when(g < groups - 1)
                 def _():
                     obs_copy_to(b, source).wait_recv()
 
@@ -570,7 +573,7 @@
                 a3[2 * q + p, at, :] = grad * sl3[2 * q + p, at, :]
         return c
 
-    lax.fori_loop(0, MR, adjoint_three, 0)
+    lax.fori_loop(0, MR, adjoint_three, 0, unroll=4)
 
     edge_rows = (0, MR - 2)
     edge_cols = (0, 2 * LW - 2)
@@ -714,7 +717,7 @@
         zbuf[pl.ds(pl.multiple_of(i * LP, 8), LP), :] = total
         return c
 
-    lax.fori_loop(0, n1, gather, 0)
+    lax.fori_loop(0, n1, gather, 0, unroll=3)
     back = zbuf[LP : LP + LR * LP] + gathered_down(window(a1, 1, LR, LP), wd1)
     zbuf[LP : LP + LR * LP] = rounded(back)
     for r in range(LR):

time: 43.7 us -> 40.8 us (0.934)
  Pallas kernels: 42.8 us -> 39.8 us
    pallas_call x1, Pallas kernels: 42.8 us -> 39.8 us  [per_device(): pl.pallas_call(functools.partial(kernel, n_lat, n_lon), out_shape=pltpu.V...]
where the time goes in v3:
time: 40.8 us; the launch traced here: 40.6 us
  Pallas kernels  39.8 us (98%)
  matrix products  0.82 us (2%)
    pallas_call x1, Pallas kernels, per_device(): pl.pallas_call(functools.partial(kernel, n_lat, n_lon), out_shape=pltpu.V...  39.8 us
    dot_general x1, matrix products, dot_nt(): lax.dot_general(x, y, (((1,), (1,)), ((), ())), preferred_element_type=F32)  0.82 us

profile of v3, /device:TPU:25, one launch (start us, length us, event | category | flops | bytes accessed | tf_op | source)
XLA Modules:
  0.0 40.6 jit_solution(18182707591539499550)
XLA Ops:
  0.0 0.0 copy-start
  0.0 39.8 %shard_map.118 = bf16[128,128]{1,0:T(8,128)(2,1)S(1)} custom-call(bf16[128,256]{1,0:T(8,128)(2,1)} %lat_hbm.1, bf16[256,128]{1,0:T(8,128)(2,1)} %inp_hbm.1, bf16[3,3,128,128]{3,2,1,0:T(8,128)(2,1)} %k1_hbm.1, bf16[3,3,128,128]{3,2,1,0:T(8,128)(2,1)} %k2_hbm.1, bf16[3,3,128,128]{3,2,1,0:T(8,128)(2,1)} %k3_hbm.1, bf16[71,128]{1,0:T(8,128)(2,1)} %bitcast.11, ...), custom_call_target="tpu_custom_call" | custom-call | flops 5000000000 | bytes 4000000 | tf_op jit(solution)/shard_map/pallas_call | solution.py:871
  39.8 0.0 copy-done
  39.8 0.8 %fusion = f32[128,256]{1,0:T(8,128)} fusion(bf16[128,128]{1,0:T(8,128)(2,1)S(1)} %shard_map.118, bf16[256,128]{1,0:T(8,128)(2,1)S(1)} %copy-done), kind=kOutput, calls=%fused_computation | convolution fusion | flops 8388608 | bytes 229376 | tf_op jit(solution)/shard_map/dot_general | solution.py:31
Async XLA Ops:
  0.0 39.8 %copy-start = (bf16[256,128]{1,0:T(8,128)(2,1)S(1)}, bf16[256,128]{1,0:T(8,128)(2,1)}, u32[]{:S(2)}) copy-start(bf16[256,128]{1,0:T(8,128)(2,1)} %inp_hbm.1) | copy-start | bytes 196612

commit v4 on v3

--- a/solution.py
+++ b/solution.py
@@ -17,7 +17,7 @@
 VP = 72
 MP = 24
 LP = 16
-S_TWO, S_HEAD, S_B3, S_B2 = 2, 1, 1, 1
+S_TWO, S_HEAD, S_B3 = 2, 1, 1
 PARTS = 4
 GUARD = 3
 HALO = [(-1, -1), (-1, 0), (-1, 1), (0, -1), (0, 1), (1, -1), (1, 0), (1, 1)]
@@ -93,8 +93,9 @@
                 for j in (n - 1, n):
                     if 0 <= i <= 2 and 0 <= j <= 2:
                         block = block + k_ref[2 - i, 2 - j].astype(F32)
-            at = (m * 4 + n) * W
-            out_ref[at : at + W, :] = block.T.astype(BF16)
+            p, near = 1 - m % 2, m in (1, 2)
+            to = 0 if near else W
+            out_ref[p, n * W : (n + 1) * W, to : to + W] = block.T.astype(BF16)
 
 
 def kernel(
@@ -189,7 +190,7 @@
     MR = 2 * LR
     npatch = (4 * LR * 4 * LW) // bank.shape[1]
     plen = bank.shape[1]
-    C_TWO, C_B3, C_B2 = (MR + 4) // S_TWO, (MR + 4) // S_B3, (MR + 4) // S_B2
+    C_TWO, C_B3 = (MR + 4) // S_TWO, (MR + 4) // S_B3
     C_HEAD = MR // S_HEAD
     nblk = patch_ref.shape[1]
     nvar = outp_ref.shape[0]
@@ -697,15 +698,26 @@
         x = jnp.concatenate([planes[m][n] for m in range(4) for n in range(4)], axis=1)
         return dot(x, weights[...])
 
-    def back_two(i, c):
-        first = i * C_B2 + GUARD - 2
-        at = pl.ds(pl.multiple_of(first * MP, 8), C_B2 * MP)
-        back = ds2[at, :] + gathered_down(window(a2, first, C_B2, MP), wd2)
-        b1[at, :] = back
-        m1[at, :] = back * sl1[at, :]
-        return c
-
-    lax.fori_loop(0, (MR + 4) // C_B2, back_two, 0)
+    def gathered_down(src, first, count, pitch, weights):
+        at = slice(first * pitch, (first + count) * pitch)
+        total = 0.0
+        for p in range(2):
+            x = jnp.concatenate(
+                [shifted(src[2 * q + p, at, :], dc).astype(BF16) for q, dc in TAPS], axis=1
+            )
+            y = dot(x, weights[p])
+            other = jnp.zeros((pitch, W), F32)
+            if p == 1:
+                other = jnp.concatenate([other, y[:-pitch, W:]], axis=0)
+            else:
+                other = jnp.concatenate([y[pitch:, W:], other], axis=0)
+            total = total + (y[:, :W] + other)
+        return total
+
+    at = slice((GUARD - 2) * MP, (GUARD + MR + 2) * MP)
+    back = ds2[at, :] + gathered_down(a2, GUARD - 2, MR + 4, MP, wd2)
+    b1[at, :] = back
+    m1[at, :] = back * sl1[at, :]
 
     def gather(i, c):
         total = jnp.zeros((LP, W), F32)
@@ -718,7 +730,7 @@
         return c
 
     lax.fori_loop(0, n1, gather, 0, unroll=3)
-    back = zbuf[LP : LP + LR * LP] + gathered_down(window(a1, 1, LR, LP), wd1)
+    back = gathered_down(a1, 0, n1, LP, wd1)[LP : LP + LR * LP] + zbuf[LP : LP + LR * LP]
     zbuf[LP : LP + LR * LP] = rounded(back)
     for r in range(LR):
         zs[r] = zbuf[(r + 1) * LP + 1 : (r + 1) * LP + 1 + LW]
@@ -820,8 +832,8 @@
         vmem((2, 6 * W, 2 * W), BF16),
         vmem((12 * W, 2 * W), BF16),
         vmem((12 * W, 2 * W), BF16),
-        vmem((16 * W, W), BF16),
-        vmem((16 * W, W), BF16),
+        vmem((2, 4 * W, 2 * W), BF16),
+        vmem((2, 4 * W, 2 * W), BF16),
         vmem((VP, W), BF16),
         vmem((VP, W), F32),
         vmem((VP, W), F32),

time: 40.8 us -> 40.1 us (0.983)
  Pallas kernels: 39.8 us -> 39.2 us
    pallas_call x1, Pallas kernels: 39.8 us -> 39.2 us  [per_device(): pl.pallas_call(functools.partial(kernel, n_lat, n_lon), out_shape=pltpu.V...]
where the time goes in v4:
time: 40.1 us; the launch traced here: 40 us
  Pallas kernels  39.2 us (98%)
  matrix products  0.82 us (2%)
    pallas_call x1, Pallas kernels, per_device(): pl.pallas_call(functools.partial(kernel, n_lat, n_lon), out_shape=pltpu.V...  39.2 us
    dot_general x1, matrix products, dot_nt(): lax.dot_general(x, y, (((1,), (1,)), ((), ())), preferred_element_type=F32)  0.82 us

profile of v4, /device:TPU:25, one launch (start us, length us, event | category | flops | bytes accessed | tf_op | source)
XLA Modules:
  0.0 40.0 jit_solution(16270817547386747109)
XLA Ops:
  0.0 0.0 copy-start
  0.0 39.2 %shard_map.118 = bf16[128,128]{1,0:T(8,128)(2,1)S(1)} custom-call(bf16[128,256]{1,0:T(8,128)(2,1)} %lat_hbm.1, bf16[256,128]{1,0:T(8,128)(2,1)} %inp_hbm.1, bf16[3,3,128,128]{3,2,1,0:T(8,128)(2,1)} %k1_hbm.1, bf16[3,3,128,128]{3,2,1,0:T(8,128)(2,1)} %k2_hbm.1, bf16[3,3,128,128]{3,2,1,0:T(8,128)(2,1)} %k3_hbm.1, bf16[71,128]{1,0:T(8,128)(2,1)} %bitcast.11, ...), custom_call_target="tpu_custom_call" | custom-call | flops 5000000000 | bytes 4000000 | tf_op jit(solution)/shard_map/pallas_call | solution.py:883
  39.2 0.0 copy-done
  39.2 0.8 %fusion = f32[128,256]{1,0:T(8,128)} fusion(bf16[128,128]{1,0:T(8,128)(2,1)S(1)} %shard_map.118, bf16[256,128]{1,0:T(8,128)(2,1)S(1)} %copy-done), kind=kOutput, calls=%fused_computation | convolution fusion | flops 8388608 | bytes 229376 | tf_op jit(solution)/shard_map/dot_general | solution.py:31
Async XLA Ops:
  0.0 39.2 %copy-start = (bf16[256,128]{1,0:T(8,128)(2,1)S(1)}, bf16[256,128]{1,0:T(8,128)(2,1)}, u32[]{:S(2)}) copy-start(bf16[256,128]{1,0:T(8,128)(2,1)} %inp_hbm.1) | copy-start | bytes 196612

commit v5 on v4

--- a/solution.py
+++ b/solution.py
@@ -303,6 +303,21 @@
     idx_copy = pltpu.make_async_copy(meta_v.at[b], idx_s, dma_sem.at[0])
     idx_copy.start()
 
+    tmp[...] = jnp.zeros_like(tmp)
+    for part in obs_parts:
+        part.wait()
+    idx_copy.wait()
+
+    def gathered(t):
+        for k in range(CAP):
+            block = pl.ds(idx_s[0, t * CAP + k], nvar, stride=nblk)
+            tmp[pl.ds(k * VP, nvar), :] = obs[block, :]
+        return tmp[...].astype(BF16)
+
+    for k in range(4):
+        if turn(0, k) < n_lon:
+            sv[after(turn(0, k))] = gathered(after(turn(0, k)))
+
     expected = (
         n_lon - 1
         + jnp.where(first_two & up, n_lon, 0)
@@ -366,16 +381,9 @@
             device_id_type=MESH,
         )
 
-    tmp[...] = jnp.zeros_like(tmp)
-    for part in obs_parts:
-        part.wait()
-    idx_copy.wait()
-
-    def gathered(t):
-        for k in range(CAP):
-            block = pl.ds(idx_s[0, t * CAP + k], nvar, stride=nblk)
-            tmp[pl.ds(k * VP, nvar), :] = obs[block, :]
-        return tmp[...].astype(BF16)
+    first = [turn(0, k) for k in range(4) if turn(0, k) < n_lon]
+    for t in first:
+        obs_copy_to(after(t), b).start()
 
     def send_obs(g, c):
         for k in range(4):
@@ -392,7 +400,7 @@
 
         return c
 
-    lax.fori_loop(0, groups, send_obs, 0)
+    lax.fori_loop(1, groups, send_obs, 0)
     rv[b] = gathered(b)
 
     for part in weight_parts:

time: 40.1 us -> 40.6 us (1.012); the launches traced: 40 us -> 40 us
  no operation moved by 1% of the time
where the time goes in v5:
time: 40.6 us; the launch traced here: 40 us
  Pallas kernels  39.2 us (97%)
  matrix products  0.82 us (2%)
    pallas_call x1, Pallas kernels, per_device(): pl.pallas_call(functools.partial(kernel, n_lat, n_lon), out_shape=pltpu.V...  39.2 us
    dot_general x1, matrix products, dot_nt(): lax.dot_general(x, y, (((1,), (1,)), ((), ())), preferred_element_type=F32)  0.82 us

profile of v5, /device:TPU:25, one launch (start us, length us, event | category | flops | bytes accessed | tf_op | source)
XLA Modules:
  0.0 40.0 jit_solution(13824106217836437562)
XLA Ops:
  0.0 0.0 copy-start
  0.0 39.2 %shard_map.118 = bf16[128,128]{1,0:T(8,128)(2,1)S(1)} custom-call(bf16[128,256]{1,0:T(8,128)(2,1)} %lat_hbm.1, bf16[256,128]{1,0:T(8,128)(2,1)} %inp_hbm.1, bf16[3,3,128,128]{3,2,1,0:T(8,128)(2,1)} %k1_hbm.1, bf16[3,3,128,128]{3,2,1,0:T(8,128)(2,1)} %k2_hbm.1, bf16[3,3,128,128]{3,2,1,0:T(8,128)(2,1)} %k3_hbm.1, bf16[71,128]{1,0:T(8,128)(2,1)} %bitcast.11, ...), custom_call_target="tpu_custom_call" | custom-call | flops 5000000000 | bytes 4000000 | tf_op jit(solution)/shard_map/pallas_call | solution.py:891
  39.2 0.0 copy-done
  39.2 0.8 %fusion = f32[128,256]{1,0:T(8,128)} fusion(bf16[128,128]{1,0:T(8,128)(2,1)S(1)} %shard_map.118, bf16[256,128]{1,0:T(8,128)(2,1)S(1)} %copy-done), kind=kOutput, calls=%fused_computation | convolution fusion | flops 8388608 | bytes 229376 | tf_op jit(solution)/shard_map/dot_general | solution.py:31
Async XLA Ops:
  0.0 39.2 %copy-start = (bf16[256,128]{1,0:T(8,128)(2,1)S(1)}, bf16[256,128]{1,0:T(8,128)(2,1)}, u32[]{:S(2)}) copy-start(bf16[256,128]{1,0:T(8,128)(2,1)} %inp_hbm.1) | copy-start | bytes 196612
